TPU v7x, 32 devices: a whole 2x2x4 slice. The times are simulated.
32 devices in a mesh: gx: 4 (over x, core), gy: 8 (over z, y).
Axes of the slice: x: 2, y: 2, z: 4, core: 2. Of those that a mesh axis runs over, the one named last changes fastest.
Arguments:
- chi: float32 [32, 32, 256], P('gy', 'gx'), may hold values from -6 to 6
- sigma: float32 [32, 32, 256], P('gy', 'gx'), may hold values from 25 to 250
- vertical: float32 [4, 64, 64], replicated, may hold values from -0.75 to 0.75
- kx: float32 [32, 32, 256], P('gy', 'gx'), may hold values from 4 to 120
- ky: float32 [32, 32, 256], P('gy', 'gx'), may hold values from 256 to 7680
Outputs:
- increment: float32 [32, 32, 256], P('gy', 'gx')
All inputs are finite; a program needn't handle non-finite values.
Results may differ from a plain program's by a relative error of at most 0.0003.
Values sent between devices are 32-bit elements; how exact they have to be, the bound alone decides.
A program may use at most 64 MiB of HBM per device.

v0:
```python
import jax
import jax.numpy as jnp
from jax import lax
from jax.sharding import PartitionSpec as P

ITERS = 3


def mobius_join(earlier, later):
    top_left = later[0] * earlier[0] + later[1] * earlier[2]
    top_right = later[0] * earlier[1] + later[1] * earlier[3]
    low_left = later[2] * earlier[0] + later[3] * earlier[2]
    low_right = later[2] * earlier[1] + later[3] * earlier[3]
    factor = 1.0 / (top_left + top_right + low_left + low_right)
    return (top_left * factor, top_right * factor, low_left * factor, low_right * factor)


def affine_join(earlier, later):
    return (earlier[0] * later[0], later[0] * earlier[1] + later[1])


def mobius_value(matrix):
    return (matrix[0] + matrix[1]) / (matrix[2] + matrix[3])


def neutral(sample):
    filled = jnp.ones_like(sample[0])
    emptied = jnp.zeros_like(sample[0])
    if len(sample) == 4:
        return (filled, emptied, emptied, filled)
    return (filled, emptied)


def settle(gathered, split, join, position):
    ups = tuple((gathered[:, member_id] for member_id in range(split)))
    downs = tuple((gathered[:, member_id] for member_id in range(split, gathered.shape[1])))
    up_scan = lax.associative_scan(join, ups, axis=0)
    down_scan = lax.associative_scan(join, downs, reverse=True, axis=0)
    up_open = neutral(tuple((member[0] for member in ups)))
    down_open = neutral(tuple((member[0] for member in downs)))
    up_in = tuple(
        (
            lax.dynamic_index_in_dim(jnp.concatenate([anchor[None], member], 0), position, 0, False)
            for anchor, member in zip(up_open, up_scan)
        )
    )
    down_in = tuple(
        (
            lax.dynamic_index_in_dim(
                jnp.concatenate([member, anchor[None]], 0), position + 1, 0, False
            )
            for anchor, member in zip(down_open, down_scan)
        )
    )
    return (up_in, down_in)


def across_x(up_total, down_total, join):
    packed = jnp.stack(up_total + down_total, 0)[None]
    gathered = lax.all_gather(packed, "gx", axis=0, tiled=True)
    return settle(gathered, len(up_total), join, lax.axis_index("gx"))


def across_y(up_total, down_total, join):
    up_in = neutral(up_total)
    down_in = neutral(down_total)
    return (up_in, down_in)


def chain(up_elements, down_elements, join, axis_dim, across):
    span = up_elements[0].shape[axis_dim]
    up_local = lax.associative_scan(join, up_elements, axis=axis_dim)
    down_local = lax.associative_scan(join, down_elements, reverse=True, axis=axis_dim)
    up_total = tuple((lax.index_in_dim(member, span - 1, axis_dim, False) for member in up_local))
    down_total = tuple((lax.index_in_dim(member, 0, axis_dim, False) for member in down_local))
    up_in, down_in = across(up_total, down_total, join)
    up_whole = join(tuple((jnp.expand_dims(member, axis_dim) for member in up_in)), up_local)
    down_whole = join(tuple((jnp.expand_dims(member, axis_dim) for member in down_in)), down_local)
    return (up_in, up_whole, down_in, down_whole)


def open_edge(conduct, axis_dim, position):
    span = conduct.shape[axis_dim]
    place = lax.broadcasted_iota(jnp.int32, conduct.shape, axis_dim) + position * span
    return jnp.where(place == 0, jnp.zeros_like(conduct), conduct)


def operator_terms(kleft, axis_dim, across):
    span = kleft.shape[axis_dim]
    matrices = (1.0 + kleft, kleft, jnp.ones_like(kleft), kleft)
    up_in, up_whole, down_in, down_whole = chain(matrices, matrices, mobius_join, axis_dim, across)
    after = mobius_value(up_whole)
    before = jnp.concatenate(
        [
            jnp.expand_dims(mobius_value(up_in), axis_dim),
            lax.slice_in_dim(after, 0, span - 1, 1, axis_dim),
        ],
        axis_dim,
    )
    behind_whole = mobius_value(down_whole)
    behind = jnp.concatenate(
        [
            lax.slice_in_dim(behind_whole, 1, span, 1, axis_dim),
            jnp.expand_dims(mobius_value(down_in), axis_dim),
        ],
        axis_dim,
    )
    return (kleft / (before + kleft), kleft / (behind + kleft), after + behind - 1.0)


def line_solve(values, terms, axis_dim, across):
    forward_rate, backward_rate, diagonal = terms
    span = values.shape[axis_dim]
    up_in, up_whole, down_in, down_whole = chain(
        (forward_rate, values),
        (backward_rate, backward_rate * values),
        affine_join,
        axis_dim,
        across,
    )
    passed = down_whole[1]
    passed_next = jnp.concatenate(
        [lax.slice_in_dim(passed, 1, span, 1, axis_dim), jnp.expand_dims(down_in[1], axis_dim)],
        axis_dim,
    )
    return (up_whole[1] + passed_next) / diagonal


def to_lines(field, partners):
    row_count = field.shape[0]
    flattened = field.reshape(row_count, -1)
    padding = -flattened.shape[1] % partners
    return jnp.pad(flattened, ((0, 0), (0, padding)))


def from_lines(lines, target_shape):
    return lines[:, : target_shape[1] * target_shape[2]].reshape(target_shape)


def body(chi, sigma, vertical, kx, ky):
    fields = vertical.shape[0]
    levels = vertical.shape[1]
    width = fields * levels
    scaled = sigma * chi
    blocks = (
        jnp.eye(fields, dtype=jnp.float32)[:, None, :, None] * vertical[:, :, None, :]
    ).reshape(width, width)
    mixed = jnp.dot(scaled.reshape(-1, width), blocks, precision=lax.Precision.HIGHEST).reshape(
        scaled.shape
    )
    x_terms = operator_terms(open_edge(kx, 1, lax.axis_index("gx")), 1, across_x)
    partners = lax.axis_size("gy")
    whole_conduct = lax.all_to_all(
        to_lines(ky, partners), "gy", split_axis=1, concat_axis=0, tiled=True
    )
    y_terms = operator_terms(open_edge(whole_conduct, 0, 0), 0, across_y)
    current = mixed
    for sweep in range(ITERS):
        current = line_solve(current, x_terms, 1, across_x)
        whole_lines = lax.all_to_all(
            to_lines(current, partners), "gy", split_axis=1, concat_axis=0, tiled=True
        )
        solved = line_solve(whole_lines, y_terms, 0, across_y)
        current = from_lines(
            lax.all_to_all(solved, "gy", split_axis=0, concat_axis=1, tiled=True), current.shape
        )
    return current


def solution(mesh):
    placed = (
        P("gy", "gx", None),
        P("gy", "gx", None),
        P(),
        P("gy", "gx", None),
        P("gy", "gx", None),
    )
    return jax.shard_map(
        body, mesh=mesh, in_specs=placed, out_specs=P("gy", "gx", None), check_vma=False
    )
```

profile of v0, /device:TPU:0, one launch (start us, length us, event | category | flops | bytes accessed | tf_op | source)
XLA Modules:
  0.0 128.1 jit_solution(2193052391039918344)
XLA Ops:
  0.0 1.4 %copy.87 = f32[4,8,256]{2,0,1:T(4,128)} copy(f32[4,8,256]{2,1,0:T(8,128)} %param.9) | data formatting | bytes 65536 | tf_op args[4]
  1.4 7.4 %all-to-all-start = ((f32[4,8,256]{2,0,1:T(4,128)}), f32[4,8,256]{2,0,1:T(4,128)S(1)}, u32[]{:S(2)}, u32[]{:S(2)}) async-start(f32[4,8,256]{2,0,1:T(4,128)} %copy.87), calls=%async_computation | async-start | bytes 65536 | tf_op jit(solution)/shard_map/all_to_all | solution.py:153
  9.6 0.1 slice.2864
  9.7 0.1 slice.2865
  12.4 0.6 slice-done.3
  13.6 5.4 %all-gather = f32[32,4,256]{2,0,1:T(8,128)S(1)} all-gather(f32[8,4,256]{2,0,1:T(8,128)S(1)} %stack.12), channel_id=2, replica_groups=mesh['gx'=4,'gy'=8] {'gx'}, dimensions={0}, use_global_device_ids=true | all-gather | bytes 163840 | tf_op jit(solution)/shard_map/all_gather | solution.py:60
  19.8 0.1 slice.2983
  19.9 0.1 slice.2986
  20.0 0.1 slice.2978
  20.1 0.1 slice.2980
  20.2 0.1 slice.2995
  20.3 0.1 slice.2993
  20.4 0.1 slice.2991
  20.5 0.1 slice.2988
  23.3 0.8 copy-done.5
  24.1 0.2 broadcast_multiply_fusion
  24.2 0.3 reshape.201
  24.7 0.7 copy-done.15
  25.4 0.2 fusion.149
  25.9 0.1 slice.3025
  26.0 0.1 slice.3039
  26.1 0.1 slice.3023
  27.1 0.1 slice.3051
  27.2 0.1 slice.3035
  28.2 5.2 %all-gather.1 = f32[16,4,256]{2,1,0:T(4,128)S(1)} all-gather(f32[4,4,256]{2,1,0:T(4,128)S(1)} %copy.112), channel_id=3, replica_groups=mesh['gx'=4,'gy'=8] {'gx'}, dimensions={0}, use_global_device_ids=true | all-gather | bytes 81920 | tf_op jit(solution)/shard_map/all_gather | solution.py:60
  33.7 0.1 slice.3080
  33.8 0.1 slice.3075
  33.9 0.1 slice.3078
  34.0 0.1 slice.3083
  34.9 0.6 copy.120
  35.5 6.0 %all-to-all-start.1 = ((f32[4,8,256]{2,0,1:T(4,128)}), f32[4,8,256]{2,0,1:T(4,128)S(1)}, u32[]{:S(2)}, u32[]{:S(2)}) async-start(f32[4,8,256]{2,0,1:T(4,128)} %copy.120), calls=%async_computation.1 | async-start | bytes 65536 | tf_op jit(solution)/shard_map/all_to_all | solution.py:160
  43.8 4.4 %all-to-all-done.1 = f32[4,8,256]{2,0,1:T(4,128)S(1)} async-done(((f32[4,8,256]{2,0,1:T(4,128)}), f32[4,8,256]{2,0,1:T(4,128)S(1)}, u32[]{:S(2)}, u32[]{:S(2)}) %all-to-all-start.1) | async-done | bytes 32800 | tf_op jit(solution)/shard_map/all_to_all | solution.py:160
  49.3 0.7 slice-done.4
  54.2 0.7 slice-done
  55.0 9.1 %all_to_all.112 = f32[8,4,256]{2,1,0:T(4,128)S(1)} all-to-all(f32[8,4,256]{2,1,0:T(4,128)S(1)} %all_to_all.90), channel_id=1, replica_groups=mesh['gx'=4,'gy'=8] {'gy'}, dimensions={0} | all-to-all | bytes 65536 | tf_op jit(solution)/shard_map/all_to_all | solution.py:165
  64.2 0.1 slice.3260
  64.9 0.1 slice.3272
  65.4 5.2 %all-gather.2 = f32[16,4,256]{2,1,0:T(4,128)S(1)} all-gather(f32[4,4,256]{2,1,0:T(4,128)S(1)} %copy.122), channel_id=4, replica_groups=mesh['gx'=4,'gy'=8] {'gx'}, dimensions={0}, use_global_device_ids=true | all-gather | bytes 81920 | tf_op jit(solution)/shard_map/all_gather | solution.py:60
  70.8 0.1 slice.3301
  70.9 0.1 slice.3296
  72.0 9.1 %all_to_all.113 = f32[4,8,256]{2,0,1:T(4,128)S(1)} all-to-all(f32[4,8,256]{2,0,1:T(4,128)S(1)} %copy.130), channel_id=1, replica_groups=mesh['gx'=4,'gy'=8] {'gy'}, dimensions={1} | all-to-all | bytes 65536 | tf_op jit(solution)/shard_map/all_to_all | solution.py:160
  81.5 0.4 copy-done.12
  82.3 0.4 copy-done.13
  82.9 0.7 slice-done.11
  83.6 0.7 slice-done.7
  84.5 0.7 slice-done.12
  85.3 0.6 slice-done.8
  86.0 0.7 slice-done.2
  86.7 9.1 %all_to_all.114 = f32[8,4,256]{2,1,0:T(4,128)S(1)} all-to-all(f32[8,4,256]{2,1,0:T(4,128)S(1)} %all_to_all.96), channel_id=1, replica_groups=mesh['gx'=4,'gy'=8] {'gy'}, dimensions={0} | all-to-all | bytes 65536 | tf_op jit(solution)/shard_map/all_to_all | solution.py:165
  97.2 5.2 %all-gather.3 = f32[16,4,256]{2,1,0:T(4,128)S(1)} all-gather(f32[4,4,256]{2,1,0:T(4,128)S(1)} %copy.132), channel_id=5, replica_groups=mesh['gx'=4,'gy'=8] {'gx'}, dimensions={0}, use_global_device_ids=true | all-gather | bytes 81920 | tf_op jit(solution)/shard_map/all_gather | solution.py:60
  102.6 0.1 slice.3415
  102.7 0.1 slice.3410
  102.8 0.1 slice.3413
  102.9 0.1 slice.3418
  103.7 9.1 %all_to_all.115 = f32[4,8,256]{2,0,1:T(4,128)S(1)} all-to-all(f32[4,8,256]{2,0,1:T(4,128)S(1)} %copy.140), channel_id=1, replica_groups=mesh['gx'=4,'gy'=8] {'gy'}, dimensions={1} | all-to-all | bytes 65536 | tf_op jit(solution)/shard_map/all_to_all | solution.py:160
  113.3 0.4 copy-done.10
  114.0 0.4 copy-done.11
  114.6 0.7 slice-done.9
  115.3 0.7 slice-done.5
  116.3 0.7 slice-done.10
  117.0 0.6 slice-done.6
  117.7 0.7 slice-done.1
  118.4 9.1 %all_to_all.116 = f32[8,4,256]{2,1,0:T(4,128)S(1)} all-to-all(f32[8,4,256]{2,1,0:T(4,128)S(1)} %all_to_all.102), channel_id=1, replica_groups=mesh['gx'=4,'gy'=8] {'gy'}, dimensions={0} | all-to-all | bytes 65536 | tf_op jit(solution)/shard_map/all_to_all | solution.py:165
  127.5 0.6 copy.141
  (1125 shorter events, 21.2 us)
Async XLA Ops:
  1.4 7.4 %copy-start.14 = (f32[4,8,256]{2,1,0:T(8,128)S(1)}, f32[4,8,256]{2,1,0:T(8,128)}, u32[]{:S(2)}) copy-start(f32[4,8,256]{2,1,0:T(8,128)} %param.8) | copy-start | bytes 98308
  1.4 34.1 %all-to-all-start = ((f32[4,8,256]{2,0,1:T(4,128)}), f32[4,8,256]{2,0,1:T(4,128)S(1)}, u32[]{:S(2)}, u32[]{:S(2)}) async-start(f32[4,8,256]{2,0,1:T(4,128)} %copy.87), calls=%async_computation | async-start | bytes 65536 | tf_op jit(solution)/shard_map/all_to_all | solution.py:153
  9.8 0.6 copy-start.3
  12.4 0.7 slice-start.3
  23.2 0.9 copy-start.5
  24.6 0.8 copy-start.15
  24.7 0.8 copy-start.16
  35.5 12.7 %all-to-all-start.1 = ((f32[4,8,256]{2,0,1:T(4,128)}), f32[4,8,256]{2,0,1:T(4,128)S(1)}, u32[]{:S(2)}, u32[]{:S(2)}) async-start(f32[4,8,256]{2,0,1:T(4,128)} %copy.120), calls=%async_computation.1 | async-start | bytes 65536 | tf_op jit(solution)/shard_map/all_to_all | solution.py:160
  41.7 1.1 copy-start.4
  48.2 4.7 %copy-start = (f32[32,256]{1,0:T(8,128)}, f32[32,256]{1,0:T(8,128)S(1)}, u32[]{:S(2)}) copy-start(f32[32,256]{1,0:T(8,128)S(1)} %all_to_all.89) | copy-start | bytes 98308
  49.3 0.7 slice-start.4
  54.1 0.7 slice-start
  81.1 1.6 %copy-start.2 = (f32[32,256]{1,0:T(8,128)}, f32[32,256]{1,0:T(8,128)S(1)}, u32[]{:S(2)}) copy-start(f32[32,256]{1,0:T(8,128)S(1)} %all_to_all.95) | copy-start | bytes 98308
  81.3 0.7 copy-start.8
  81.3 0.6 copy-start.12
  82.0 0.7 copy-start.9
  82.1 0.6 copy-start.13
  82.8 0.7 slice-start.11
  83.6 0.7 slice-start.7
  84.5 0.7 slice-start.12
  85.2 0.7 slice-start.8
  85.9 0.7 slice-start.2
  112.8 1.6 %copy-start.1 = (f32[32,256]{1,0:T(8,128)}, f32[32,256]{1,0:T(8,128)S(1)}, u32[]{:S(2)}) copy-start(f32[32,256]{1,0:T(8,128)S(1)} %all_to_all.101) | copy-start | bytes 98308
  113.0 0.7 copy-start.6
  113.1 0.6 copy-start.10
  113.8 0.7 copy-start.7
  113.8 0.6 copy-start.11
  114.6 0.7 slice-start.9
  115.3 0.7 slice-start.5
  116.2 0.7 slice-start.10
  117.0 0.7 slice-start.6
  117.7 0.7 slice-start.1
where the time goes:
time: 129 us; the launch traced here: 128 us
  blocking collectives  66.5 us (52%)
  local copies, waits for them, and re-layouts  33 us (26%)
  starting transfers between devices  13.4 us (10%)
  other arithmetic  5.67 us (4%)
  between operations  5 us (4%)
  waiting for transfers between devices  4.36 us (3%)
    all_to_all x3, blocking collectives, body(): lax.all_to_all(solved, 'gy', split_axis=0, concat_axis=1, tiled=True)  27.2 us
    all_gather x4, blocking collectives, across_x(): gathered = lax.all_gather(packed, 'gx', axis=0, tiled=True)  21.2 us
    all_to_all x2, blocking collectives, body(): lax.all_to_all(to_lines(current, partners), 'gy', split_axis=1, concat_ax...  18.1 us
    slice x176, local copies, waits for them, and re-layouts, chain(): lax.associative_scan(join, down_elements, reverse=True, axis=axis_dim)  8.88 us
    all_to_all x1, starting transfers between devices, body(): lax.all_to_all(to_lines(ky, partners), 'gy', split_axis=1, concat_axis=0,...  7.41 us
    slice x151, local copies, waits for them, and re-layouts, chain(): up_local = lax.associative_scan(join, up_elements, axis=axis_dim)  7.02 us
    all_to_all x1, starting transfers between devices, body(): lax.all_to_all(to_lines(current, partners), 'gy', split_axis=1, concat_ax...  6 us
    unnamed x63, local copies, waits for them, and re-layouts  4.73 us
  transfers between devices with their start and end apart: 2, of which 1 were waited for; matrix products, arithmetic and copies ran while one was open for 11% of the time, Pallas kernels for 0%

commit v1 on v0

--- a/solution.py
+++ b/solution.py
@@ -1,6 +1,10 @@
+import functools
+
 import jax
 import jax.numpy as jnp
 from jax import lax
+from jax.experimental import pallas as pl
+from jax.experimental.pallas import tpu as pltpu
 from jax.sharding import PartitionSpec as P
 
 ITERS = 3
@@ -167,7 +171,239 @@
     return current
 
 
+LANES = 128
+SUBLANES = 8
+
+
+def channels_fit(shape, split_x, split_y):
+    rows, span, width = shape
+    return (
+        span == SUBLANES
+        and rows * span * split_x == LANES
+        and split_x >= 3
+        and width == SUBLANES * split_x * split_y
+        and rows & (rows - 1) == 0
+        and split_x & (split_x - 1) == 0
+        and split_y & (split_y - 1) == 0
+    )
+
+
+def reduction_rates(kleft, length, below, above):
+    excess = jnp.ones_like(kleft)
+    west = kleft
+    east = above(kleft, 1)
+    rates = []
+    stride = 1
+    while stride < length:
+        inverse = 1.0 / (excess + west + east)
+        from_below = west * below(inverse, stride)
+        from_above = east * above(inverse, stride)
+        excess = excess + from_below * below(excess, stride) + from_above * above(excess, stride)
+        west = from_below * below(west, stride)
+        east = from_above * above(east, stride)
+        rates.append((stride, from_below, from_above))
+        stride *= 2
+    return rates, 1.0 / excess
+
+
+def reduced_solve(values, operator, below, above):
+    rates, inverse = operator
+    for stride, from_below, from_above in rates:
+        values = values + from_below * below(values, stride) + from_above * above(values, stride)
+    return values * inverse
+
+
+def channel_kernel(
+    split_x,
+    split_y,
+    chi_ref,
+    sigma_ref,
+    vertical_ref,
+    kx_ref,
+    ky_ref,
+    out_ref,
+    staged,
+    sent,
+    got,
+    solved,
+    back,
+    turned,
+    send_sem,
+    recv_sem,
+    back_send_sem,
+    back_recv_sem,
+):
+    rows, span, width = chi_ref.shape
+    fields, levels, _ = vertical_ref.shape
+    count = split_x * split_y
+    length_x = split_x * span
+    length_y = split_y * rows
+    gx, gy = (lax.axis_index("gx"), lax.axis_index("gy"))
+    me = gy * split_x + gx
+
+    def peer_at(step):
+        peer = lax.rem(me + step, count)
+        return peer, peer // split_x, lax.rem(peer, split_x)
+
+    barrier = pltpu.get_barrier_semaphore()
+    for step in range(1, count):
+        _, peer_y, peer_x = peer_at(step)
+        pl.semaphore_signal(
+            barrier,
+            inc=1,
+            device_id={"gx": peer_x, "gy": peer_y},
+            device_id_type=pl.DeviceIdType.MESH,
+        )
+
+    scaled = (sigma_ref[...] * chi_ref[...]).reshape(rows * span, width)
+    mixed = jnp.concatenate(
+        [
+            jnp.dot(
+                scaled[:, f * levels : (f + 1) * levels],
+                vertical_ref[f],
+                precision=lax.Precision.HIGHEST,
+                preferred_element_type=jnp.float32,
+            )
+            for f in range(fields)
+        ],
+        1,
+    )
+
+    def place(turn, row, tile):
+        block = row * split_x + lax.rem(gx + turn, split_x)
+        staged[pl.ds(pl.multiple_of(block * span, span), span), :] = tile
+
+    for row in range(rows):
+        place(0, row, mixed[row * span : (row + 1) * span])
+        place(1, row, kx_ref[row])
+        place(2, row, ky_ref[row])
+        for turn in range(3, split_x):
+            place(turn, row, jnp.zeros((span, width), jnp.float32))
+    sent[...] = staged[...].T.reshape(sent.shape)
+
+    pl.semaphore_wait(barrier, count - 1)
+    for step in range(1, count):
+        peer, peer_y, peer_x = peer_at(step)
+        pltpu.make_async_remote_copy(
+            src_ref=sent.at[peer],
+            dst_ref=got.at[me],
+            send_sem=send_sem,
+            recv_sem=recv_sem,
+            device_id={"gx": peer_x, "gy": peer_y},
+            device_id_type=pl.DeviceIdType.MESH,
+        ).start()
+    got[me] = sent[me]
+    others = pl.ds(0, count - 1)
+    pltpu.make_async_copy(got.at[others], got.at[others], recv_sem).wait()
+
+    lane = lax.broadcasted_iota(jnp.int32, (split_y * SUBLANES, LANES), 1)
+    tile_row = lax.broadcasted_iota(jnp.int32, (split_y * SUBLANES, LANES), 0)
+    cell_x = lane % length_x
+    block_x = cell_x // span
+    tiles = got[...].reshape(split_y, split_x, SUBLANES, LANES)
+    sources = [tiles[:, g].reshape(split_y * SUBLANES, LANES) for g in range(split_x)]
+
+    def collect(turn):
+        whole = sources[0]
+        for g in range(1, split_x):
+            whole = jnp.where(block_x == (g + turn) % split_x, sources[g], whole)
+        if turn:
+            ahead = pltpu.roll(whole, LANES - turn * span, 1)
+            wrapped = pltpu.roll(whole, length_x - turn * span, 1)
+            whole = jnp.where(cell_x < length_x - turn * span, ahead, wrapped)
+        return whole
+
+    def tiles_on(values, tiles_by):
+        moved = (tiles_by % split_y) * SUBLANES
+        if moved == 0:
+            return values
+        return jnp.concatenate([values[-moved:], values[:-moved]], 0)
+
+    def below_x(values, stride):
+        return pltpu.roll(values, stride, 1)
+
+    def above_x(values, stride):
+        return pltpu.roll(values, LANES - stride, 1)
+
+    def below_y(values, stride):
+        if stride >= rows:
+            return tiles_on(values, stride // rows)
+        lanes = stride * length_x
+        turned_by = pltpu.roll(values, lanes, 1)
+        return jnp.where(lane < lanes, tiles_on(turned_by, 1), turned_by)
+
+    def above_y(values, stride):
+        if stride >= rows:
+            return tiles_on(values, -(stride // rows))
+        lanes = stride * length_x
+        turned_by = pltpu.roll(values, LANES - lanes, 1)
+        return jnp.where(lane >= LANES - lanes, tiles_on(turned_by, -1), turned_by)
+
+    field = collect(0)
+    west = jnp.where(cell_x == 0, 0.0, collect(1))
+    south = jnp.where((tile_row < SUBLANES) & (lane < length_x), 0.0, collect(2))
+    x_operator = reduction_rates(west, length_x, below_x, above_x)
+    y_operator = reduction_rates(south, length_y, below_y, above_y)
+    for sweep in range(ITERS):
+        field = reduced_solve(field, x_operator, below_x, above_x)
+        field = reduced_solve(field, y_operator, below_y, above_y)
+    solved[...] = field.reshape(solved.shape)
+
+    for step in range(1, count):
+        peer, peer_y, peer_x = peer_at(step)
+        pltpu.make_async_remote_copy(
+            src_ref=solved.at[peer_y],
+            dst_ref=back.at[me],
+            send_sem=back_send_sem,
+            recv_sem=back_recv_sem,
+            device_id={"gx": peer_x, "gy": peer_y},
+            device_id_type=pl.DeviceIdType.MESH,
+        ).start()
+    back[me] = solved[gy]
+    pltpu.make_async_copy(back.at[others], back.at[others], back_recv_sem).wait()
+    turned[...] = back[...].reshape(count * SUBLANES, LANES).T
+    for row in range(rows):
+        start = pl.multiple_of((row * split_x + gx) * span, span)
+        out_ref[row] = turned[pl.ds(start, span), :]
+    pltpu.make_async_copy(sent.at[others], sent.at[others], send_sem).wait()
+    pltpu.make_async_copy(back.at[others], back.at[others], back_send_sem).wait()
+
+
+def channel_body(split_x, split_y, chi, sigma, vertical, kx, ky):
+    rows, span, width = chi.shape
+    count = split_x * split_y
+    whole = pl.BlockSpec(memory_space=pltpu.VMEM)
+    return pl.pallas_call(
+        functools.partial(channel_kernel, split_x, split_y),
+        out_shape=jax.ShapeDtypeStruct(chi.shape, jnp.float32),
+        in_specs=[whole] * 5,
+        out_specs=whole,
+        scratch_shapes=[
+            pltpu.VMEM((LANES, width), jnp.float32),
+            pltpu.VMEM((count, SUBLANES, LANES), jnp.float32),
+            pltpu.VMEM((count, SUBLANES, LANES), jnp.float32),
+            pltpu.VMEM((split_y, SUBLANES, LANES), jnp.float32),
+            pltpu.VMEM((count, SUBLANES, LANES), jnp.float32),
+            pltpu.VMEM((LANES, width), jnp.float32),
+            pltpu.SemaphoreType.DMA,
+            pltpu.SemaphoreType.DMA,
+            pltpu.SemaphoreType.DMA,
+            pltpu.SemaphoreType.DMA,
+        ],
+        compiler_params=pltpu.CompilerParams(collective_id=0, has_side_effects=True),
+        name="channel_lines",
+    )(chi, sigma, vertical, kx, ky)
+
+
 def solution(mesh):
+    split_x, split_y = (mesh.shape["gx"], mesh.shape["gy"])
+
+    def chosen(chi, sigma, vertical, kx, ky):
+        if channels_fit(chi.shape, split_x, split_y):
+            return channel_body(split_x, split_y, chi, sigma, vertical, kx, ky)
+        return body(chi, sigma, vertical, kx, ky)
+
+
     placed = (
         P("gy", "gx", None),
         P("gy", "gx", None),
@@ -176,5 +412,5 @@
         P("gy", "gx", None),
     )
     return jax.shard_map(
-        body, mesh=mesh, in_specs=placed, out_specs=P("gy", "gx", None), check_vma=False
-    )
+        chosen, mesh=mesh, in_specs=placed, out_specs=P("gy", "gx", None), check_vma=False
+    )

time: 129 us -> 22.6 us (0.18)
  blocking collectives: 66.5 us -> 0 us
  local copies, waits for them, and re-layouts: 33 us -> 1.38 us
  Pallas kernels: 0 us -> 21.1 us
  starting transfers between devices: 13.4 us -> 0 us
  other arithmetic: 5.67 us -> 0 us
  between operations: 5 us -> 0.01 us
  waiting for transfers between devices: 4.36 us -> 0 us
    all_to_all x5 -> x0, blocking collectives: 45.3 us -> none  [the longest x3 27.2 us: body(): lax.all_to_all(solved, 'gy', split_axis=0, concat_axis=1, tiled=True)]
    all_gather x4 -> x0, blocking collectives: 21.2 us -> none  [across_x(): gathered = lax.all_gather(packed, 'gx', axis=0, tiled=True)]
    pallas_call x0 -> x1, Pallas kernels: none -> 21.1 us  [channel_body(): pl.pallas_call(functools.partial(channel_kernel, split_x, split_y), out_s...]
    slice x380 -> x0, local copies, waits for them, and re-layouts: 18.8 us -> none  [the longest x176 8.88 us: chain(): lax.associative_scan(join, down_elements, reverse=True, axis=axis_dim)]
    all_to_all x2 -> x0, starting transfers between devices: 13.4 us -> none  [the longest x1 7.41 us: body(): lax.all_to_all(to_lines(ky, partners), 'gy', split_axis=1, concat_axis=0,...]
    pad x220 -> x0, local copies, waits for them, and re-layouts: 5.52 us -> none  [the longest x96 2.06 us: chain(): lax.associative_scan(join, down_elements, reverse=True, axis=axis_dim)]
    all_to_all x2 -> x0, waiting for transfers between devices: 4.36 us -> none  [the longest x1 4.35 us: body(): lax.all_to_all(to_lines(current, partners), 'gy', split_axis=1, concat_ax...]
    unnamed x63 -> x1, local copies, waits for them, and re-layouts: 4.73 us -> 1.38 us
  transfers between devices with their start and end apart: 2 -> 0, of which waited for: 1 -> 0; matrix products, arithmetic and copies ran while one was open for 11% -> 0% of each run, Pallas kernels for 0% -> 0%
where the time goes in v1:
time: 22.6 us; the launch traced here: 22.5 us
  Pallas kernels  21.1 us (93%)
  local copies, waits for them, and re-layouts  1.38 us (6%)
    pallas_call x1, Pallas kernels, channel_body(): pl.pallas_call(functools.partial(channel_kernel, split_x, split_y), out_s...  21.1 us
    unnamed x1, local copies, waits for them, and re-layouts  1.38 us

profile of v1, /device:TPU:0, one launch (start us, length us, event | category | flops | bytes accessed | tf_op | source)
XLA Modules:
  0.0 22.5 jit_solution(11424817978076056525)
XLA Ops:
  0.0 21.1 %channel_lines.1 = f32[4,8,256]{2,1,0:T(8,128)} custom-call(f32[4,8,256]{2,1,0:T(8,128)} %chi_ref.1, f32[4,8,256]{2,1,0:T(8,128)} %sigma_ref.1, f32[4,64,64]{2,1,0:T(8,128)} %vertical_ref.1, f32[4,8,256]{2,1,0:T(8,128)} %kx_ref.1, f32[4,8,256]{2,1,0:T(8,128)} %ky_ref.1), custom_call_target="tpu_custom_call" | custom-call | tf_op jit(solution)/shard_map/channel_lines/pallas_call | solution.py:376
  21.1 1.4 %copy.7 = f32[4,8,256]{2,1,0:T(8,128)} copy(f32[4,8,256]{2,1,0:T(8,128)} %channel_lines.1) | data formatting | bytes 65536
